TPU v7x, 32 devices: a whole 2x2x4 slice. The times are simulated.
32 devices in a mesh: row: 4 (over y, x), col: 8 (over z, core).
Axes of the slice: x: 2, y: 2, z: 4, core: 2. Of those that a mesh axis runs over, the one named last changes fastest.
Arguments:
- intensity: int32 [128, 2048], P('row', 'col'), may hold values from 0 to 255
- agreement: int32 [4, 128, 2048], P(None, 'row', 'col'), may hold values from 0 to 8
- basis_block: float32 [128, 128, 2048], P(None, 'row', 'col'), may hold values from -2000 to 2000
Outputs:
- ortho_block: float32 [128, 128, 2048], P(None, 'row', 'col')
- upper_factor: float32 [128, 128], replicated
All inputs are finite; a program needn't handle non-finite values.
Results may differ from a plain program's by a relative error of at most 0.00014.
Values sent between devices are 32-bit elements; how exact they have to be, the bound alone decides.
A program may use at most 64 MiB of HBM per device.

v0:
```python
import jax
import jax.numpy as jnp
from jax import lax
from jax.experimental import pallas as pl
from jax.experimental.pallas import tpu as pltpu
from jax.sharding import PartitionSpec as P

INV_SIGMA = 1.0 / 40.0
NEIGHBOURS = (
    (0, 1, 0, 1, 1.0 / 9.0),
    (0, -1, 0, 0, 1.0 / 9.0),
    (1, 0, 1, 1, 1.0 / 9.0),
    (-1, 0, 1, 0, 1.0 / 9.0),
    (1, 1, 2, 1, 1.0 / 18.0),
    (-1, -1, 2, 0, 1.0 / 18.0),
    (1, -1, 3, 1, 1.0 / 18.0),
    (-1, 1, 3, 0, 1.0 / 18.0),
)
PANEL = 16


def padded(cells, sides, width):
    for axis, dim in sides:
        count = lax.axis_size(axis)
        ends = count - 1
        head = lax.slice_in_dim(cells, 0, width, axis=dim)
        tail = lax.slice_in_dim(cells, cells.shape[dim] - width, cells.shape[dim], axis=dim)
        cells = jnp.concatenate(
            [
                lax.ppermute(tail, axis, [(i, (i + 1) % count) for i in range(ends)]),
                cells,
                lax.ppermute(head, axis, [((i + 1) % count, i) for i in range(ends)]),
            ],
            axis=dim,
        )
    return cells


def shifted(array, step_row, step_col):
    height = array.shape[-2]
    width = array.shape[-1]
    return array[..., 1 + step_row : height - 1 + step_row, 1 + step_col : width - 1 + step_col]


def cropped(array, cycle):
    return array[..., cycle:-cycle, cycle:-cycle]


def neighbour_weights(levels, counts, inside):
    center = shifted(levels, 0, 0)
    center_in = shifted(inside, 0, 0)
    result = []
    for step_row, step_col, channel, at_center, factor in NEIGHBOURS:
        other = shifted(levels, step_row, step_col)
        if at_center == 1:
            source = shifted(counts[channel], 0, 0)
        else:
            source = shifted(counts[channel], step_row, step_col)
        gap = (center - other) * INV_SIGMA
        result.append(
            (1.0 + source)
            * factor
            * jnp.exp(-gap * gap)
            * center_in
            * shifted(inside, step_row, step_col)
        )
    return result


def degree_scales(weights):
    degree = weights[0]
    for weight in weights[1:]:
        degree = degree + weight
    return lax.rsqrt(1.0 + degree)


def apply_once(values_in, weights, scales):
    lifted = values_in * scales
    summed = None
    for weight, entry in zip(weights, NEIGHBOURS):
        term = weight * shifted(lifted, entry[0], entry[1])
        summed = term if summed is None else summed + term
    return shifted(values_in, 0, 0) - shifted(scales, 0, 0) * summed


def inner_products(first_mat, second_mat):
    return jnp.dot(
        first_mat, second_mat.T, precision=lax.Precision.HIGHEST, preferred_element_type=jnp.float32
    )


def factor_panels(work):
    size, width = work.shape
    for base in range(0, size, PANEL):
        block = work[pl.ds(base, PANEL), :]
        rows = [block[i : i + 1, :] for i in range(PANEL)]
        pivots = [
            [
                None
                if k < i
                else jnp.broadcast_to(rows[i][:, base + k : base + k + 1], (1, width))
                for k in range(PANEL)
            ]
            for i in range(PANEL)
        ]
        for i in range(PANEL):
            inverse = lax.rsqrt(pivots[i][i])
            rows[i] = rows[i] * inverse
            lead = [None if k <= i else pivots[i][k] * inverse for k in range(PANEL)]
            for k in range(i + 1, PANEL):
                for m in range(k, PANEL):
                    pivots[k][m] = pivots[k][m] - lead[k] * lead[m]
            for k in range(i + 1, PANEL):
                rows[k] = rows[k] - lead[k] * rows[i]
        done = jnp.concatenate(rows, axis=0)
        work[pl.ds(base, PANEL), :] = done
        rest = size - base - PANEL
        if rest > 0:
            change = lax.dot_general(
                done[:, :size].T,
                done,
                (((1,), (0,)), ((), ())),
                precision=lax.Precision.HIGHEST,
                preferred_element_type=jnp.float32,
            )
            work[pl.ds(base + PANEL, rest), :] = (
                work[pl.ds(base + PANEL, rest), :] - change[base + PANEL :, :]
            )


def split_two(values):
    high = values.astype(jnp.bfloat16)
    low = (values - high.astype(jnp.float32)).astype(jnp.bfloat16)
    return high, low


def ortho_kernel(scale, gram_ref, filt_ref, ortho_ref, upper_ref, work, filt, out, in_sem, out_sem):
    size = gram_ref.shape[0]
    rows = filt.shape[0]
    fetch = pltpu.make_async_copy(filt_ref, filt, in_sem)
    fetch.start()
    row_id = lax.broadcasted_iota(jnp.int32, (size, size), 0)
    col_id = lax.broadcasted_iota(jnp.int32, (size, size), 1)
    work[:, :size] = gram_ref[...] * scale
    work[:, size:] = jnp.where(row_id == col_id, 1.0, 0.0).astype(jnp.float32)
    factor_panels(work)
    upper_ref[...] = jnp.where(row_id <= col_id, work[:, :size], 0.0)
    high, low = split_two(work[:, size:])
    left = jnp.concatenate(
        [jnp.concatenate([high, high], axis=1), jnp.concatenate([low, low], axis=1)], axis=0
    )
    fetch.wait()
    sends = []
    for group in range(rows // 8):
        parts = []
        for r in range(8):
            pair = jnp.concatenate(split_two(filt[group * 8 + r]), axis=0)
            both = jnp.dot(left, pair, preferred_element_type=jnp.float32)
            parts.append(both[:size] + both[size:])
        out[:, pl.ds(group * 8, 8), :] = jnp.swapaxes(jnp.stack(parts, axis=0), 0, 1)
        send = pltpu.make_async_copy(
            out.at[:, pl.ds(group * 8, 8), :],
            ortho_ref.at[:, pl.ds(group * 8, 8), :],
            out_sem.at[group],
        )
        send.start()
        sends.append(send)
    for send in sends:
        send.wait()


def ortho_call(gram, filt, pixels):
    rows, vectors, cols = filt.shape

    def body(*refs):
        ortho_kernel(1.0 / pixels, *refs)

    return pl.pallas_call(
        body,
        out_shape=(
            jax.ShapeDtypeStruct((vectors, rows, cols), jnp.float32),
            jax.ShapeDtypeStruct((vectors, vectors), jnp.float32),
        ),
        in_specs=[
            pl.BlockSpec(memory_space=pltpu.VMEM),
            pl.BlockSpec(memory_space=pl.ANY),
        ],
        out_specs=(
            pl.BlockSpec(memory_space=pl.ANY),
            pl.BlockSpec(memory_space=pltpu.VMEM),
        ),
        scratch_shapes=[
            pltpu.VMEM((vectors, 2 * vectors), jnp.float32),
            pltpu.VMEM((rows, vectors, cols), filt.dtype),
            pltpu.VMEM((vectors, rows, cols), jnp.float32),
            pltpu.SemaphoreType.DMA,
            pltpu.SemaphoreType.DMA((rows // 8,)),
        ],
        compiler_params=pltpu.CompilerParams(vmem_limit_bytes=40 * 1024 * 1024),
        name="ortho",
    )(gram, filt)


def per_device(intensity, agreement, basis_block):
    vectors, tile_rows, tile_cols = basis_block.shape
    row_count = lax.axis_size("row")
    col_count = lax.axis_size("col")
    total_rows = tile_rows * row_count
    total_cols = tile_cols * col_count
    labels = jnp.concatenate((intensity[None], agreement), axis=0)
    labels_wide = padded(labels, (("row", 1), ("col", 2)), 3)
    row_ids = lax.axis_index("row") * tile_rows + jnp.arange(-3, tile_rows + 3, dtype=jnp.int32)
    col_ids = lax.axis_index("col") * tile_cols + jnp.arange(-3, tile_cols + 3, dtype=jnp.int32)
    row_in = ((row_ids >= 0) & (row_ids < total_rows)).astype(jnp.float32)
    col_in = ((col_ids >= 0) & (col_ids < total_cols)).astype(jnp.float32)
    inside = row_in[:, None] * col_in[None, :]
    levels = labels_wide[0].astype(jnp.float32)
    counts = labels_wide[1:].astype(jnp.float32)
    weights = neighbour_weights(levels, counts, inside)
    scales = degree_scales(weights)
    cycle_zero = [cropped(weight, 2) for weight in weights]
    filtered = basis_block
    for repeat in range(2):
        extended = padded(filtered, (("row", 1), ("col", 2)), 1)
        filtered = apply_once(extended, cycle_zero, cropped(scales, 1))
    flat = filtered.reshape(vectors, tile_rows * tile_cols)
    gram = lax.psum(inner_products(flat, flat), ("row", "col"))
    return ortho_call(gram, filtered.swapaxes(0, 1), float(total_rows * total_cols))


def solution(mesh):
    return jax.shard_map(
        per_device,
        mesh=mesh,
        in_specs=(P("row", "col"), P(None, "row", "col"), P(None, "row", "col")),
        out_specs=(P(None, "row", "col"), P()),
        check_vma=False,
    )
```

profile of v0, /device:TPU:0, one launch (start us, length us, event | category | flops | bytes accessed | tf_op | source)
XLA Modules:
  0.0 294.0 jit_solution(14584092686686981234)
XLA Ops:
  8.0 4.8 %collective-permute-start = (s32[5,3,256]{2,1,0:T(4,128)S(1)}, s32[5,3,256]{2,1,0:T(4,128)S(1)}, u32[]{:S(2)}, u32[]{:S(2)}) collective-permute-start(s32[5,3,256]{2,1,0:T(4,128)S(1)} %get-tuple-element.25), channel_id=1, source_target_pairs={{0,8},{8,16},{16,24},{1,9},{9,17},{17,25},{2,10},{10,18},{18,26},{... | collective-permute-start | bytes 46088 | tf_op jit(solution)/shard_map/ppermute | solution.py:30
  12.9 1.3 collective-permute-start.1
  14.2 1.7 fusion.82
  15.9 4.6 %collective-permute-start.4 = (f32[128,1,256]{2,0,1:T(8,128)S(1)}, f32[128,1,256]{2,0,1:T(8,128)S(1)}, u32[]{:S(2)}, u32[]{:S(2)}) collective-permute-start(f32[128,1,256]{2,0,1:T(8,128)S(1)} %copy.23), channel_id=1, source_target_pairs={{0,8},{8,16},{16,24},{1,9},{9,17},{17,25},{2,10},{10,18},{18,26},{... | collective-permute-start | bytes 393224 | tf_op jit(solution)/shard_map/ppermute | solution.py:30
  20.5 1.3 collective-permute-start.5
  22.9 1.3 collective-permute-start.2
  25.6 3.6 %collective-permute-done.3 = s32[5,38,3]{2,1,0:T(8,128)S(1)} collective-permute-done((s32[5,38,3]{2,1,0:T(8,128)S(1)}, s32[5,38,3]{2,1,0:T(8,128)S(1)}, u32[]{:S(2)}, u32[]{:S(2)}) %collective-permute-start.3) | collective-permute-done | bytes 2312 | tf_op jit(solution)/shard_map/ppermute | solution.py:32
  31.3 4.9 %constant_dynamic-update-slice_fusion.1 = f32[128,34,256]{2,0,1:T(8,128)S(1)} fusion(f32[128,34,256]{2,0,1:T(8,128)S(1)} %constant_dynamic-update-slice_fusion.2, f32[128,32,256]{2,1,0:T(8,128)} %param.5), kind=kLoop, calls=%fused_computation.124 | loop fusion | bytes 8388608
  36.2 2.6 fusion.80
  38.9 2.3 copy.12
  41.9 1.3 collective-permute-start.7
  43.2 6.0 %collective-permute-start.6 = (f32[128,34,1]{0,2,1:T(1,128)S(1)}, f32[128,34,1]{0,2,1:T(1,128)S(1)}, u32[]{:S(2)}, u32[]{:S(2)}) collective-permute-start(f32[128,34,1]{0,2,1:T(1,128)S(1)} %copy.12), channel_id=1, source_target_pairs={{0,1},{1,2},{2,3},{3,4},{4,5},{5,6},{6,7},{8,9},{9,10},{10,11},{11... | collective-permute-start | bytes 52232 | tf_op jit(solution)/shard_map/ppermute | solution.py:30
  51.1 2.1 copy.15
  53.1 6.8 %maximum_multiply_fusion = f32[128,34,258]{2,0,1:T(8,128)} fusion(f32[128,34,1]{2,0,1:T(8,128)} %copy.15, f32[128,34,256]{2,0,1:T(8,128)} %copy-done.2, f32[128,34,1]{2,0,1:T(8,128)S(1)} %copy.14, f32[34,258]{1,0:T(8,128)S(1)} %slice.326), kind=kLoop, calls=%fused_computation | loop fusion | flops 3368448 | bytes 9017616 | tf_op jit(solution)/shard_map/mul | solution.py:78
  59.9 23.6 %fusion.11 = f32[128,32,256]{2,0,1:T(8,128)} fusion(f32[128,34,258]{2,0,1:T(8,128)} %maximum_multiply_fusion, f32[32,256]{1,0:T(8,128)S(1)} %slice.340, f32[32,256]{1,0:T(8,128)S(1)} %slice.338, f32[32,256]{1,0:T(8,128)S(1)} %slice.336, f32[32,256]{1,0:T(8,128)S(1)} %slice.334, f32[32,256]{1,0:T(8,128)S(1)} %slice.332, f32[32,256]{1,0:T(8,128)S(1)} %slice.330, ...), kind=kLoop, calls=%fused_computation.23 | loop fusion | flops 17825792 | bytes 42237952 | tf_op jit(solution)/shard_map/sub | solution.py:83
  84.4 4.9 %collective-permute-start.8 = (f32[128,1,256]{2,0,1:T(8,128)S(1)}, f32[128,1,256]{2,0,1:T(8,128)S(1)}, u32[]{:S(2)}, u32[]{:S(2)}) collective-permute-start(f32[128,1,256]{2,0,1:T(8,128)S(1)} %get-tuple-element.15), channel_id=1, source_target_pairs={{0,8},{8,16},{16,24},{1,9},{9,17},{17,25},{2,10},{10,18},{18,26},{... | collective-permute-start | bytes 393224 | tf_op jit(solution)/shard_map/ppermute | solution.py:30
  89.4 1.3 collective-permute-start.9
  90.7 1.8 collective-permute-done.8
  92.5 6.2 %collective-permute-done.9 = f32[128,1,256]{2,0,1:T(8,128)S(1)} collective-permute-done((f32[128,1,256]{2,0,1:T(8,128)S(1)}, f32[128,1,256]{2,0,1:T(8,128)S(1)}, u32[]{:S(2)}, u32[]{:S(2)}) %collective-permute-start.9) | collective-permute-done | bytes 131104 | tf_op jit(solution)/shard_map/ppermute | solution.py:32
  98.7 2.7 pad_maximum_fusion
  101.4 2.2 fusion.79
  103.6 2.3 copy.17
  105.8 2.5 collective-permute-start.10
  109.0 1.5 collective-permute-start.11
  111.2 3.0 %collective-permute-done.11 = f32[128,34,1]{0,2,1:T(1,128)S(1)} collective-permute-done((f32[128,34,1]{0,2,1:T(1,128)S(1)}, f32[128,34,1]{0,2,1:T(1,128)S(1)}, u32[]{:S(2)}, u32[]{:S(2)}) %collective-permute-start.11) | collective-permute-done | bytes 17440 | tf_op jit(solution)/shard_map/ppermute | solution.py:32
  114.2 2.1 copy.20
  116.3 7.6 %maximum_multiply_fusion.1 = f32[128,34,258]{2,0,1:T(8,128)} fusion(f32[128,34,1]{2,0,1:T(8,128)} %copy.20, f32[128,1,256]{2,0,1:T(8,128)S(1)} %collective-permute-done.9, f32[128,32,256]{2,0,1:T(8,128)} %fusion.11, f32[128,1,256]{2,0,1:T(8,128)S(1)} %collective-permute-done.8, f32[128,34,1]{2,0,1:T(8,128)S(1)} %copy.19, f32[34,258]{1,0:T(8,128)S(1)} %slice.326), kind=kLoop, calls=%fused_computation.1 | loop fusion | flops 5614080 | bytes 9017616 | tf_op jit(solution)/shard_map/mul | solution.py:78
  123.9 23.1 %fusion.2 = f32[128,32,256]{2,0,1:T(8,128)} fusion(f32[128,32,256]{2,0,1:T(8,128)} %fusion.11, f32[128,34,258]{2,0,1:T(8,128)} %maximum_multiply_fusion.1, f32[32,256]{1,0:T(8,128)S(1)} %slice.340, f32[32,256]{1,0:T(8,128)S(1)} %slice.338, f32[32,256]{1,0:T(8,128)S(1)} %slice.336, f32[32,256]{1,0:T(8,128)S(1)} %slice.334, f32[32,256]{1,0:T(8,128)S(1)} %slice.332, ...), kind=kLoop, calls=%fused_computation.6 | loop fusion | flops 17825792 | bytes 42237952 | tf_op jit(solution)/shard_map/sub | solution.py:83
  147.0 7.6 %convolution_bitcast_fusion = f32[128,128]{1,0:T(8,128)} fusion(f32[128,32,256]{2,0,1:T(8,128)} %fusion.2), kind=kOutput, calls=%fused_computation.37 | convolution fusion | flops 1610612736 | bytes 4259840 | tf_op jit(solution)/shard_map/dot_general | solution.py:87
  154.6 119.3 %all-reduce.2.cloned.1.call-done.refs_0_ = f32[128,128]{1,0:T(8,128)} async-done(((f32[128,128]{1,0:T(8,128)}), f32[128,128]{1,0:T(8,128)}) %all-reduce.2.cloned.1.call-update) | async-done | bytes 65552 | tf_op jit(solution)/shard_map/psum | solution.py:227
  274.0 2.2 copy-done
  277.0 10.2 %ortho.1 = (f32[128,32,256]{2,1,0:T(8,128)}, f32[128,128]{1,0:T(8,128)}) custom-call(f32[128,128]{1,0:T(8,128)S(1)} %copy-done.1, f32[32,128,256]{2,1,0:T(8,128)S(1)} %bitcast.16), custom_call_target="tpu_custom_call" | custom-call | tf_op jit(solution)/shard_map/ortho/pallas_call | solution.py:178
  (46 shorter events, 11.1 us)
Async XLA Ops:
  7.2 266.8 %all-reduce.2.cloned.1.call-start = ((), (), s32[]{:S(2)}) async-start(), calls=%async_computation | async-start | bytes 131072 | tf_op jit(solution)/shard_map/psum | solution.py:227
  8.0 13.8 %collective-permute-start = (s32[5,3,256]{2,1,0:T(4,128)S(1)}, s32[5,3,256]{2,1,0:T(4,128)S(1)}, u32[]{:S(2)}, u32[]{:S(2)}) collective-permute-start(s32[5,3,256]{2,1,0:T(4,128)S(1)} %get-tuple-element.25), channel_id=1, source_target_pairs={{0,8},{8,16},{16,24},{1,9},{9,17},{17,25},{2,10},{10,18},{18,26},{... | collective-permute-start | bytes 46088 | tf_op jit(solution)/shard_map/ppermute | solution.py:30
  12.9 9.0 %collective-permute-start.1 = (s32[5,3,256]{2,1,0:T(4,128)S(1)}, s32[5,3,256]{2,1,0:T(4,128)S(1)}, u32[]{:S(2)}, u32[]{:S(2)}) collective-permute-start(s32[5,3,256]{2,1,0:T(4,128)S(1)} %get-tuple-element.26), channel_id=1, source_target_pairs={{8,0},{16,8},{24,16},{9,1},{17,9},{25,17},{10,2},{18,10},{26,18},{... | collective-permute-start | bytes 46088 | tf_op jit(solution)/shard_map/ppermute | solution.py:32
  15.9 15.3 %collective-permute-start.4 = (f32[128,1,256]{2,0,1:T(8,128)S(1)}, f32[128,1,256]{2,0,1:T(8,128)S(1)}, u32[]{:S(2)}, u32[]{:S(2)}) collective-permute-start(f32[128,1,256]{2,0,1:T(8,128)S(1)} %copy.23), channel_id=1, source_target_pairs={{0,8},{8,16},{16,24},{1,9},{9,17},{17,25},{2,10},{10,18},{18,26},{... | collective-permute-start | bytes 393224 | tf_op jit(solution)/shard_map/ppermute | solution.py:30
  20.5 15.7 %collective-permute-start.5 = (f32[128,1,256]{2,0,1:T(8,128)S(1)}, f32[128,1,256]{2,0,1:T(8,128)S(1)}, u32[]{:S(2)}, u32[]{:S(2)}) collective-permute-start(f32[128,1,256]{2,0,1:T(8,128)S(1)} %copy.24), channel_id=1, source_target_pairs={{8,0},{16,8},{24,16},{9,1},{17,9},{25,17},{10,2},{18,10},{26,18},{... | collective-permute-start | bytes 393224 | tf_op jit(solution)/shard_map/ppermute | solution.py:32
  22.9 2.7 collective-permute-start.2
  24.2 5.0 %collective-permute-start.3 = (s32[5,38,3]{2,1,0:T(8,128)S(1)}, s32[5,38,3]{2,1,0:T(8,128)S(1)}, u32[]{:S(2)}, u32[]{:S(2)}) collective-permute-start(s32[5,38,3]{2,1,0:T(8,128)S(1)} %get-tuple-element.24), channel_id=1, source_target_pairs={{1,0},{2,1},{3,2},{4,3},{5,4},{6,5},{7,6},{9,8},{10,9},{11,10},{12... | collective-permute-start | bytes 6848 | tf_op jit(solution)/shard_map/ppermute | solution.py:32
  36.2 2.8 copy-start.2
  41.9 9.2 %collective-permute-start.7 = (f32[128,34,1]{0,2,1:T(1,128)S(1)}, f32[128,34,1]{0,2,1:T(1,128)S(1)}, u32[]{:S(2)}, u32[]{:S(2)}) collective-permute-start(f32[128,34,1]{0,2,1:T(1,128)S(1)} %copy.13), channel_id=1, source_target_pairs={{1,0},{2,1},{3,2},{4,3},{5,4},{6,5},{7,6},{9,8},{10,9},{11,10},{12... | collective-permute-start | bytes 52232 | tf_op jit(solution)/shard_map/ppermute | solution.py:32
  43.2 7.2 %collective-permute-start.6 = (f32[128,34,1]{0,2,1:T(1,128)S(1)}, f32[128,34,1]{0,2,1:T(1,128)S(1)}, u32[]{:S(2)}, u32[]{:S(2)}) collective-permute-start(f32[128,34,1]{0,2,1:T(1,128)S(1)} %copy.12), channel_id=1, source_target_pairs={{0,1},{1,2},{2,3},{3,4},{4,5},{5,6},{6,7},{8,9},{9,10},{10,11},{11... | collective-permute-start | bytes 52232 | tf_op jit(solution)/shard_map/ppermute | solution.py:30
  84.4 8.1 %collective-permute-start.8 = (f32[128,1,256]{2,0,1:T(8,128)S(1)}, f32[128,1,256]{2,0,1:T(8,128)S(1)}, u32[]{:S(2)}, u32[]{:S(2)}) collective-permute-start(f32[128,1,256]{2,0,1:T(8,128)S(1)} %get-tuple-element.15), channel_id=1, source_target_pairs={{0,8},{8,16},{16,24},{1,9},{9,17},{17,25},{2,10},{10,18},{18,26},{... | collective-permute-start | bytes 393224 | tf_op jit(solution)/shard_map/ppermute | solution.py:30
  89.4 9.3 %collective-permute-start.9 = (f32[128,1,256]{2,0,1:T(8,128)S(1)}, f32[128,1,256]{2,0,1:T(8,128)S(1)}, u32[]{:S(2)}, u32[]{:S(2)}) collective-permute-start(f32[128,1,256]{2,0,1:T(8,128)S(1)} %get-tuple-element.16), channel_id=1, source_target_pairs={{8,0},{16,8},{24,16},{9,1},{17,9},{25,17},{10,2},{18,10},{26,18},{... | collective-permute-start | bytes 393224 | tf_op jit(solution)/shard_map/ppermute | solution.py:32
  105.8 4.6 %collective-permute-start.10 = (f32[128,34,1]{0,2,1:T(1,128)S(1)}, f32[128,34,1]{0,2,1:T(1,128)S(1)}, u32[]{:S(2)}, u32[]{:S(2)}) collective-permute-start(f32[128,34,1]{0,2,1:T(1,128)S(1)} %copy.17), channel_id=1, source_target_pairs={{0,1},{1,2},{2,3},{3,4},{4,5},{5,6},{6,7},{8,9},{9,10},{10,11},{11... | collective-permute-start | bytes 52232 | tf_op jit(solution)/shard_map/ppermute | solution.py:30
  109.0 5.2 %collective-permute-start.11 = (f32[128,34,1]{0,2,1:T(1,128)S(1)}, f32[128,34,1]{0,2,1:T(1,128)S(1)}, u32[]{:S(2)}, u32[]{:S(2)}) collective-permute-start(f32[128,34,1]{0,2,1:T(1,128)S(1)} %copy.18), channel_id=1, source_target_pairs={{1,0},{2,1},{3,2},{4,3},{5,4},{6,5},{7,6},{9,8},{10,9},{11,10},{12... | collective-permute-start | bytes 52232 | tf_op jit(solution)/shard_map/ppermute | solution.py:32
  273.9 2.2 copy-start
  276.1 0.8 copy-start.1
Sparse Core Ops, SparseCore 0:
  154.7 119.1 all-reduce.1
where the time goes:
time: 296 us; the launch traced here: 294 us
  waiting for transfers between devices  134 us (45%)
  other arithmetic  67.9 us (23%)
  starting transfers between devices  32.1 us (11%)
  local copies, waits for them, and re-layouts  27.9 us (9%)
  between operations  14.4 us (5%)
  Pallas kernels  10.2 us (3%)
  matrix products  7.58 us (3%)
    psum x1, waiting for transfers between devices, per_device(): gram = lax.psum(inner_products(flat, flat), ('row', 'col'))  119 us
    sub x2, other arithmetic, apply_once(): return shifted(values_in, 0, 0) - shifted(scales, 0, 0) * summed  46.7 us
    ppermute x6, starting transfers between devices, padded(): lax.ppermute(tail, axis, [(i, (i + 1) % count) for i in range(ends)])  24.1 us
    mul x2, other arithmetic, apply_once(): lifted = values_in * scales  14.4 us
    ppermute x6, waiting for transfers between devices, padded(): lax.ppermute(head, axis, [((i + 1) % count, i) for i in range(ends)])  12.8 us
    slice x6, local copies, waits for them, and re-layouts, padded(): lax.slice_in_dim(cells, cells.shape[dim] - width, cells.shape[dim], axis=...  10.4 us
    pallas_call x1, Pallas kernels, ortho_call(): pl.pallas_call(body, out_shape=(jax.ShapeDtypeStruct((vectors, rows, cols...  10.2 us
    unnamed x10, local copies, waits for them, and re-layouts  8.1 us
  transfers between devices with their start and end apart: 13, of which 5 were waited for; matrix products, arithmetic and copies ran while one was open for 4% of the time, Pallas kernels for 0%

commit v1 on v0

v1 whole, which is shorter than its diff:
```python
import jax
import jax.numpy as jnp
from jax import lax
from jax.experimental import pallas as pl
from jax.experimental.pallas import tpu as pltpu
from jax.sharding import PartitionSpec as P

INV_SIGMA = 1.0 / 40.0
NEIGHBOURS = (
    (0, 1, 0, 1, 1.0 / 9.0),
    (0, -1, 0, 0, 1.0 / 9.0),
    (1, 0, 1, 1, 1.0 / 9.0),
    (-1, 0, 1, 0, 1.0 / 9.0),
    (1, 1, 2, 1, 1.0 / 18.0),
    (-1, -1, 2, 0, 1.0 / 18.0),
    (1, -1, 3, 1, 1.0 / 18.0),
    (-1, 1, 3, 0, 1.0 / 18.0),
)
PANEL = 16


DIRECTIONS = ((-1, 0), (1, 0), (0, -1), (0, 1), (-1, -1), (-1, 1), (1, -1), (1, 1))
STEPS = ((-1, -1), (0, -1), (1, -1), (-1, 1), (0, 1), (1, 1), (-1, 0), (1, 0))
CHUNK = 16
LANES = 128
EDGE = 8


def moved(array, step_row, step_col):
    height, width = array.shape
    if step_row:
        array = pltpu.roll(array, (-step_row) % height, 0)
    if step_col:
        array = pltpu.roll(array, (-step_col) % width, 1)
    return array


def stencil_weights(levels_ref, counts_ref, weights, row, col, row_count, col_count):
    height, width = levels_ref.shape
    rows, cols = height - 2 * EDGE, width - 2 * LANES
    row_id = lax.broadcasted_iota(jnp.int32, (height, width), 0) - EDGE + row * rows
    col_id = lax.broadcasted_iota(jnp.int32, (height, width), 1) - LANES + col * cols
    total_rows, total_cols = rows * row_count, cols * col_count

    def is_inside(step_row, step_col):
        r, c = row_id + step_row, col_id + step_col
        return (r >= 0) & (r < total_rows) & (c >= 0) & (c < total_cols)

    center_in = is_inside(0, 0)
    levels = levels_ref[...].astype(jnp.float32)
    edges = {}
    for step_row, step_col, channel, at_center, factor in NEIGHBOURS:
        if at_center == 1:
            gap = (levels - moved(levels, step_row, step_col)) * INV_SIGMA
            count = counts_ref[channel].astype(jnp.float32)
            weight = (1.0 + count) * factor * jnp.exp(-gap * gap)
            edges[channel] = (
                jnp.where(center_in & is_inside(step_row, step_col), weight, 0.0),
                (step_row, step_col),
            )
    degree = None
    for step_row, step_col, channel, at_center, factor in NEIGHBOURS:
        weight = edges[channel][0]
        if at_center == 0:
            weight = moved(weight, step_row, step_col)
        degree = weight if degree is None else degree + weight
    scales = lax.rsqrt(1.0 + degree)
    table = {}
    for step_row, step_col, channel, at_center, factor in NEIGHBOURS:
        if at_center == 1:
            scaled = edges[channel][0] * scales * moved(scales, step_row, step_col)
            table[(step_row, step_col)] = scaled
            table[(-step_row, -step_col)] = moved(scaled, -step_row, -step_col)
    lane = lax.broadcasted_iota(jnp.int32, (height, LANES), 1)
    for n, (step_row, step_col) in enumerate(STEPS):
        weight = moved(table[(step_row, step_col)], 0, -step_col)
        weights[n, :, :cols] = weight[:, LANES : LANES + cols]
        weights[n, :, cols:] = jnp.where(
            lane < LANES // 2, weight[:, LANES + cols :], weight[:, :LANES]
        )


def apply_row(source, at, weights, weight_row, store):
    vectors, width = source.shape[1], source.shape[2]
    parts = [weights[n, pl.ds(weight_row, 1), :] for n in range(len(STEPS))]
    for base in range(0, vectors, CHUNK):
        above = source[at - 1, base : base + CHUNK, :]
        here = source[at, base : base + CHUNK, :]
        below = source[at + 1, base : base + CHUNK, :]
        from_left = parts[0] * above + parts[1] * here + parts[2] * below
        from_right = parts[3] * above + parts[4] * here + parts[5] * below
        upright = parts[6] * above + parts[7] * below
        store(
            base,
            here - (upright + pltpu.roll(from_left, 1, 1) + pltpu.roll(from_right, width - 1, 1)),
        )


def filter_kernel(
    row_count,
    col_count,
    levels_in,
    counts_in,
    basis_in,
    pair_out,
    gram_out,
    levels,
    counts,
    natural,
    wide,
    middle,
    weights,
    packed,
    halo,
    pairs,
    total,
    share,
    landed,
    blocks,
    whole,
    local_sem,
    send_sem,
    recv_sem,
    sum_send,
    sum_recv,
):
    vectors, rows, cols = natural.shape
    width = cols + LANES
    row, col = lax.axis_index("row"), lax.axis_index("col")

    def device(step_row, step_col):
        return {
            "row": jnp.clip(row + step_row, 0, row_count - 1),
            "col": jnp.clip(col + step_col, 0, col_count - 1),
        }

    def exists(step_row, step_col):
        r, c = row + step_row, col + step_col
        return (r >= 0) & (r < row_count) & (c >= 0) & (c < col_count)

    groups = rows // 8
    order = [0, groups - 1] + list(range(1, groups - 1))
    fetches = {}
    for g in order:
        fetches[g] = pltpu.make_async_copy(
            basis_in.at[:, pl.ds(8 * g, 8), :],
            natural.at[:, pl.ds(8 * g, 8), :],
            local_sem.at[g],
        )
        fetches[g].start()
    own = [
        pltpu.make_async_copy(
            levels_in, levels.at[pl.ds(EDGE, rows), pl.ds(LANES, cols)], local_sem.at[groups]
        ),
        pltpu.make_async_copy(
            counts_in, counts.at[:, pl.ds(EDGE, rows), pl.ds(LANES, cols)], local_sem.at[groups + 1]
        ),
    ]
    for copy in own:
        copy.start()
    zeros = jnp.zeros((2, vectors, cols), jnp.float32)
    wide[0:2, :, :cols] = zeros
    wide[rows + 2 : rows + 4, :, :cols] = zeros
    halo[...] = jnp.zeros(halo.shape, jnp.float32)

    barrier = pltpu.get_barrier_semaphore()

    def greet(target):
        pl.semaphore_signal(
            barrier, inc=1, device_id=target, device_id_type=pl.DeviceIdType.MESH
        )

    for off in range(1, col_count):
        greet({"row": row, "col": lax.rem(col + off, col_count)})
    for off in range(1, row_count):
        greet({"row": lax.rem(row + off, row_count), "col": col})
    corners = jnp.int32(0)
    for step in DIRECTIONS[4:]:
        corners = corners + jnp.where(exists(*step), 1, 0)

        @pl.when(exists(*step))
        def _(step=step):
            greet(device(*step))

    pl.semaphore_wait(barrier, col_count + row_count - 2 + corners)

    def span(step, size, edge):
        if step == 0:
            return 0, edge, size
        if step == 1:
            return size - edge, 0, edge
        return 0, edge + size, edge

    def remote(source, target, kind, d):
        return pltpu.make_async_remote_copy(
            src_ref=source,
            dst_ref=target,
            send_sem=send_sem.at[kind, d],
            recv_sem=recv_sem.at[kind, d],
            device_id=device(*DIRECTIONS[d]),
            device_id_type=pl.DeviceIdType.MESH,
        )

    def launch(d, copies):
        @pl.when(exists(*DIRECTIONS[d]))
        def _():
            for copy in copies:
                copy.start()

    def arrive(d, copies):
        @pl.when(exists(-DIRECTIONS[d][0], -DIRECTIONS[d][1]))
        def _():
            for copy in copies:
                copy.wait_recv()

    label_copies = []
    for d, (step_row, step_col) in enumerate(DIRECTIONS):
        r_from, r_to, r_len = span(step_row, rows, EDGE)
        c_from, c_to, c_len = span(step_col, cols, LANES)
        label_copies.append(
            [
                remote(
                    levels_in.at[pl.ds(r_from, r_len), pl.ds(c_from, c_len)],
                    levels.at[pl.ds(r_to, r_len), pl.ds(c_to, c_len)],
                    0,
                    d,
                ),
                remote(
                    counts_in.at[:, pl.ds(r_from, r_len), pl.ds(c_from, c_len)],
                    counts.at[:, pl.ds(r_to, r_len), pl.ds(c_to, c_len)],
                    1,
                    d,
                ),
            ]
        )
        launch(d, label_copies[d])

    def turn(g):
        fetches[g].wait()
        wide[pl.ds(2 + 8 * g, 8), :, pl.ds(0, cols)] = jnp.swapaxes(
            natural[:, pl.ds(8 * g, 8), :], 0, 1
        )

    turn(0)
    value_copies = [None] * 8
    value_copies[0] = [
        remote(wide.at[pl.ds(2, 2), :, pl.ds(0, cols)],
               wide.at[pl.ds(rows + 2, 2), :, pl.ds(0, cols)], 2, 0)
    ]
    launch(0, value_copies[0])
    turn(groups - 1)
    value_copies[1] = [
        remote(wide.at[pl.ds(rows, 2), :, pl.ds(0, cols)],
               wide.at[pl.ds(0, 2), :, pl.ds(0, cols)], 2, 1)
    ]
    launch(1, value_copies[1])
    for g in range(1, groups - 1):
        turn(g)

    lane = lax.broadcasted_iota(jnp.int32, (vectors, LANES), 1)
    used = 2 * rows
    for side, start in ((0, 0), (1, cols - LANES)):
        gathered = jnp.zeros((vectors, LANES), jnp.float32)
        for r in range(rows):
            strip = wide[2 + r, :, start : start + LANES]
            shift = (2 * r + 2 * side) % LANES
            if shift:
                strip = pltpu.roll(strip, shift, 1)
            gathered = jnp.where(lane // 2 == r, strip, gathered)
        packed[side] = gathered.T
    for d, (step_row, step_col) in enumerate(DIRECTIONS):
        if step_col == 0:
            continue
        side = 0 if step_col < 0 else 1
        p_from, p_to, p_len = span(step_row, used, EDGE)
        value_copies[d] = [
            remote(
                packed.at[side, pl.ds(p_from, p_len), :],
                halo.at[1 - side, pl.ds(p_to, p_len), :],
                2,
                d,
            )
        ]
        launch(d, value_copies[d])

    for copy in own:
        copy.wait()
    for d in range(8):
        arrive(d, label_copies[d])
    stencil_weights(levels, counts, weights, row, col, row_count, col_count)

    for d in range(2, 8):
        arrive(d, value_copies[d])
    left, right = halo[0].T, halo[1].T
    for r in range(-2, rows + 2):
        on_right = pltpu.roll(right, (-(EDGE + 2 * r)) % LANES, 1)
        on_left = pltpu.roll(left, (LANES - 2 - EDGE - 2 * r) % LANES, 1)
        wide[2 + r, :, cols:] = jnp.where(lane < LANES // 2, on_right, on_left)

    def first(m):
        def store(base, values):
            middle[m, base : base + CHUNK, :] = values

        apply_row(wide, m + 1, weights, m + EDGE - 1, store)

    def second(r):
        def store(base, values):
            high, low = split_two(values[:, :cols])
            pairs[r, base : base + CHUNK, :] = high
            pairs[r, vectors + base : vectors + base + CHUNK, :] = low

        apply_row(middle, r + 1, weights, r + EDGE, store)

    def product(r):
        pair = pairs[r]
        total[...] += lax.dot_general(
            pair, pair, (((1,), (1,)), ((), ())), preferred_element_type=jnp.float32
        )

    total[...] = jnp.zeros(total.shape, jnp.float32)
    first(2)
    first(3)

    def inner(r, carry):
        first(r + 2)
        second(r)
        return carry

    lax.fori_loop(2, rows - 2, inner, 0)

    def inner_product(r, carry):
        product(r)
        return carry

    lax.fori_loop(2, rows - 2, inner_product, 0)
    for d in range(2):
        arrive(d, value_copies[d])
    for m in (0, 1, rows, rows + 1):
        first(m)
    for r in (0, 1, rows - 2, rows - 1):
        second(r)
    keep = pltpu.make_async_copy(pairs, pair_out, local_sem.at[groups + 2])
    keep.start()
    for r in (0, 1, rows - 2, rows - 1):
        product(r)

    block = vectors // col_count
    share[...] = (total[:vectors, :vectors] + total[vectors:, vectors:]) + (
        total[:vectors, vectors:] + total[vectors:, :vectors]
    )

    def swap(source, target, n, peer):
        copy = pltpu.make_async_remote_copy(
            src_ref=source,
            dst_ref=target,
            send_sem=sum_send.at[n],
            recv_sem=sum_recv.at[n],
            device_id=peer,
            device_id_type=pl.DeviceIdType.MESH,
        )
        copy.start()
        return copy

    def col_peer(off):
        return {"row": row, "col": lax.rem(col + off, col_count)}

    scatter = []
    for off in range(1, col_count):
        place = pl.multiple_of(lax.rem(col + off, col_count) * block, block)
        scatter.append(
            swap(share.at[pl.ds(place, block), :], landed.at[off], off - 1, col_peer(off))
        )
    mine = pl.multiple_of(col * block, block)
    part = share[pl.ds(mine, block), :]
    for off in range(1, col_count):
        scatter[off - 1].wait_recv()
        part = part + landed[off]
    blocks[row] = part
    spread = []
    for off in range(1, row_count):
        spread.append(
            swap(
                blocks.at[row],
                blocks.at[row],
                col_count + off - 1,
                {"row": lax.rem(row + off, row_count), "col": col},
            )
        )
    for copy in spread:
        copy.wait_recv()
    part = blocks[0]
    for n in range(1, row_count):
        part = part + blocks[n]
    whole[pl.ds(mine, block), :] = part
    collect = []
    for off in range(1, col_count):
        collect.append(
            swap(
                whole.at[pl.ds(mine, block), :],
                whole.at[pl.ds(mine, block), :],
                col_count + row_count + off - 1,
                col_peer(off),
            )
        )
    for copy in collect:
        copy.wait_recv()
    gram_out[...] = whole[...]
    for d in range(8):

        @pl.when(exists(*DIRECTIONS[d]))
        def _(d=d):
            for copy in label_copies[d] + value_copies[d]:
                copy.wait_send()

    for copy in scatter + spread + collect:
        copy.wait_send()
    keep.wait()


def filter_call(intensity, agreement, basis_block, row_count, col_count):
    vectors, rows, cols = basis_block.shape
    block = vectors // col_count

    def body(*refs):
        filter_kernel(row_count, col_count, *refs)

    any_spec = pl.BlockSpec(memory_space=pl.ANY)
    f32 = jnp.float32
    swaps = 2 * col_count + row_count
    return pl.pallas_call(
        body,
        out_shape=(
            jax.ShapeDtypeStruct((rows, 2 * vectors, cols), jnp.bfloat16),
            jax.ShapeDtypeStruct((vectors, vectors), f32),
        ),
        in_specs=[any_spec] * 3,
        out_specs=(any_spec, pl.BlockSpec(memory_space=pltpu.VMEM)),
        scratch_shapes=[
            pltpu.VMEM((rows + 2 * EDGE, cols + 2 * LANES), jnp.int32),
            pltpu.VMEM((4, rows + 2 * EDGE, cols + 2 * LANES), jnp.int32),
            pltpu.VMEM((vectors, rows, cols), f32),
            pltpu.VMEM((rows + 4, vectors, cols + LANES), f32),
            pltpu.VMEM((rows + 2, vectors, cols + LANES), f32),
            pltpu.VMEM((len(STEPS), rows + 2 * EDGE, cols + LANES), f32),
            pltpu.VMEM((2, LANES, vectors), f32),
            pltpu.VMEM((2, LANES, vectors), f32),
            pltpu.VMEM((rows, 2 * vectors, cols), jnp.bfloat16),
            pltpu.VMEM((2 * vectors, 2 * vectors), f32),
            pltpu.VMEM((vectors, vectors), f32),
            pltpu.VMEM((col_count, block, vectors), f32),
            pltpu.VMEM((row_count, block, vectors), f32),
            pltpu.VMEM((vectors, vectors), f32),
            pltpu.SemaphoreType.DMA((rows // 8 + 3,)),
            pltpu.SemaphoreType.DMA((3, 8)),
            pltpu.SemaphoreType.DMA((3, 8)),
            pltpu.SemaphoreType.DMA((swaps,)),
            pltpu.SemaphoreType.DMA((swaps,)),
        ],
        compiler_params=pltpu.CompilerParams(
            collective_id=0, has_side_effects=True, vmem_limit_bytes=48 * 1024 * 1024
        ),
        name="filter",
    )(intensity, agreement, basis_block)


def factor_panels(work):
    size, width = work.shape
    for base in range(0, size, PANEL):
        block = work[pl.ds(base, PANEL), :]
        rows = [block[i : i + 1, :] for i in range(PANEL)]
        pivots = [
            [
                None
                if k < i
                else jnp.broadcast_to(rows[i][:, base + k : base + k + 1], (1, width))
                for k in range(PANEL)
            ]
            for i in range(PANEL)
        ]
        for i in range(PANEL):
            inverse = lax.rsqrt(pivots[i][i])
            rows[i] = rows[i] * inverse
            lead = [None if k <= i else pivots[i][k] * inverse for k in range(PANEL)]
            for k in range(i + 1, PANEL):
                for m in range(k, PANEL):
                    pivots[k][m] = pivots[k][m] - lead[k] * lead[m]
            for k in range(i + 1, PANEL):
                rows[k] = rows[k] - lead[k] * rows[i]
        done = jnp.concatenate(rows, axis=0)
        work[pl.ds(base, PANEL), :] = done
        rest = size - base - PANEL
        if rest > 0:
            change = lax.dot_general(
                done[:, :size].T,
                done,
                (((1,), (0,)), ((), ())),
                precision=lax.Precision.HIGHEST,
                preferred_element_type=jnp.float32,
            )
            work[pl.ds(base + PANEL, rest), :] = (
                work[pl.ds(base + PANEL, rest), :] - change[base + PANEL :, :]
            )


def split_two(values):
    high = values.astype(jnp.bfloat16)
    low = (values - high.astype(jnp.float32)).astype(jnp.bfloat16)
    return high, low


def ortho_kernel(scale, gram_ref, filt_ref, ortho_ref, upper_ref, work, filt, out, in_sem, out_sem):
    size = gram_ref.shape[0]
    rows = filt.shape[0]
    fetch = pltpu.make_async_copy(filt_ref, filt, in_sem)
    fetch.start()
    row_id = lax.broadcasted_iota(jnp.int32, (size, size), 0)
    col_id = lax.broadcasted_iota(jnp.int32, (size, size), 1)
    work[:, :size] = gram_ref[...] * scale
    work[:, size:] = jnp.where(row_id == col_id, 1.0, 0.0).astype(jnp.float32)
    factor_panels(work)
    upper_ref[...] = jnp.where(row_id <= col_id, work[:, :size], 0.0)
    high, low = split_two(work[:, size:])
    left = jnp.concatenate(
        [jnp.concatenate([high, high], axis=1), jnp.concatenate([low, low], axis=1)], axis=0
    )
    fetch.wait()
    sends = []
    for group in range(rows // 8):
        parts = []
        for r in range(8):
            both = jnp.dot(left, filt[group * 8 + r], preferred_element_type=jnp.float32)
            parts.append(both[:size] + both[size:])
        out[:, pl.ds(group * 8, 8), :] = jnp.swapaxes(jnp.stack(parts, axis=0), 0, 1)
        send = pltpu.make_async_copy(
            out.at[:, pl.ds(group * 8, 8), :],
            ortho_ref.at[:, pl.ds(group * 8, 8), :],
            out_sem.at[group],
        )
        send.start()
        sends.append(send)
    for send in sends:
        send.wait()


def ortho_call(gram, filt, pixels):
    vectors = gram.shape[0]
    rows, _, cols = filt.shape

    def body(*refs):
        ortho_kernel(1.0 / pixels, *refs)

    return pl.pallas_call(
        body,
        out_shape=(
            jax.ShapeDtypeStruct((vectors, rows, cols), jnp.float32),
            jax.ShapeDtypeStruct((vectors, vectors), jnp.float32),
        ),
        in_specs=[
            pl.BlockSpec(memory_space=pltpu.VMEM),
            pl.BlockSpec(memory_space=pl.ANY),
        ],
        out_specs=(
            pl.BlockSpec(memory_space=pl.ANY),
            pl.BlockSpec(memory_space=pltpu.VMEM),
        ),
        scratch_shapes=[
            pltpu.VMEM((vectors, 2 * vectors), jnp.float32),
            pltpu.VMEM(filt.shape, filt.dtype),
            pltpu.VMEM((vectors, rows, cols), jnp.float32),
            pltpu.SemaphoreType.DMA,
            pltpu.SemaphoreType.DMA((rows // 8,)),
        ],
        compiler_params=pltpu.CompilerParams(vmem_limit_bytes=40 * 1024 * 1024),
        name="ortho",
    )(gram, filt)


def per_device(intensity, agreement, basis_block):
    vectors, tile_rows, tile_cols = basis_block.shape
    row_count = lax.axis_size("row")
    col_count = lax.axis_size("col")
    total_rows = tile_rows * row_count
    total_cols = tile_cols * col_count
    pairs, gram = filter_call(intensity, agreement, basis_block, row_count, col_count)
    return ortho_call(gram, pairs, float(total_rows * total_cols))


def solution(mesh):
    return jax.shard_map(
        per_device,
        mesh=mesh,
        in_specs=(P("row", "col"), P(None, "row", "col"), P(None, "row", "col")),
        out_specs=(P(None, "row", "col"), P()),
        check_vma=False,
    )
```

time: 296 us -> 64.5 us (0.22)
  waiting for transfers between devices: 134 us -> 0 us
  other arithmetic: 67.9 us -> 0 us
  Pallas kernels: 10.2 us -> 61.9 us
  starting transfers between devices: 32.1 us -> 0 us
  local copies, waits for them, and re-layouts: 27.9 us -> 1.65 us
  between operations: 14.4 us -> 0.81 us
  matrix products: 7.58 us -> 0 us
    psum x1 -> x0, waiting for transfers between devices: 119 us -> none  [per_device(): gram = lax.psum(inner_products(flat, flat), ('row', 'col'))]
    pallas_call x0 -> x1, Pallas kernels: none -> 52.1 us  [filter_call(): pl.pallas_call(body, out_shape=(jax.ShapeDtypeStruct((rows, 2 * vectors,...]
    sub x2 -> x0, other arithmetic: 46.7 us -> none  [apply_once(): return shifted(values_in, 0, 0) - shifted(scales, 0, 0) * summed]
    ppermute x12 -> x0, starting transfers between devices: 32.1 us -> none  [the longest x6 24.1 us: padded(): lax.ppermute(tail, axis, [(i, (i + 1) % count) for i in range(ends)])]
    ppermute x12 -> x0, waiting for transfers between devices: 14.7 us -> none  [the longest x6 12.8 us: padded(): lax.ppermute(head, axis, [((i + 1) % count, i) for i in range(ends)])]
    mul x3 -> x0, other arithmetic: 14.4 us -> none  [the longest x2 14.4 us: apply_once(): lifted = values_in * scales]
    slice x19 -> x0, local copies, waits for them, and re-layouts: 14.3 us -> none  [the longest x6 10.4 us: padded(): lax.slice_in_dim(cells, cells.shape[dim] - width, cells.shape[dim], axis=...]
    dot_general x1 -> x0, matrix products: 7.58 us -> none  [inner_products(): jnp.dot(first_mat, second_mat.T, precision=lax.Precision.HIGHEST, preferr...]
  transfers between devices with their start and end apart: 13 -> 0, of which waited for: 5 -> 0; matrix products, arithmetic and copies ran while one was open for 4% -> 0% of each run, Pallas kernels for 0% -> 0%
where the time goes in v1:
time: 64.5 us; the launch traced here: 64.3 us
  Pallas kernels  61.9 us (96%)
  local copies, waits for them, and re-layouts  1.65 us (3%)
  between operations  0.81 us (1%)
    pallas_call x1, Pallas kernels, filter_call(): pl.pallas_call(body, out_shape=(jax.ShapeDtypeStruct((rows, 2 * vectors,...  52.1 us
    pallas_call x1, Pallas kernels, ortho_call(): pl.pallas_call(body, out_shape=(jax.ShapeDtypeStruct((vectors, rows, cols...  9.81 us
    unnamed x4, local copies, waits for them, and re-layouts  1.65 us

profile of v1, /device:TPU:0, one launch (start us, length us, event | category | flops | bytes accessed | tf_op | source)
XLA Modules:
  0.0 64.3 jit_solution(16830743162712329204)
XLA Ops:
  0.6 0.0 copy-start
  0.6 0.9 %copy-done = s32[4,32,256]{2,1,0:T(8,128)S(1)} copy-done((s32[4,32,256]{2,1,0:T(8,128)S(1)}, s32[4,32,256]{2,1,0:T(8,128)}, u32[]{:S(2)}) %copy-start) | copy-done | bytes 131096
  1.5 0.0 copy-start.1
  1.5 0.8 %copy-done.1 = s32[32,256]{1,0:T(8,128)S(1)} copy-done((s32[32,256]{1,0:T(8,128)S(1)}, s32[32,256]{1,0:T(8,128)}, u32[]{:S(2)}) %copy-start.1) | copy-done | bytes 32792
  2.3 52.1 %filter.1 = (bf16[32,256,256]{2,1,0:T(8,128)(2,1)S(1)}, f32[128,128]{1,0:T(8,128)S(1)}) custom-call(s32[32,256]{1,0:T(8,128)S(1)} %copy-done.1, s32[4,32,256]{2,1,0:T(8,128)S(1)} %copy-done, f32[128,32,256]{2,1,0:T(8,128)} %refs_2_.1), custom_call_target="tpu_custom_call" | custom-call | tf_op jit(solution)/shard_map/filter/pallas_call | solution.py:430
  54.4 9.8 %ortho.1 = (f32[128,32,256]{2,1,0:T(8,128)}, f32[128,128]{1,0:T(8,128)}) custom-call(f32[128,128]{1,0:T(8,128)S(1)} %get-tuple-element.4.refs_0_, bf16[32,256,256]{2,1,0:T(8,128)(2,1)S(1)} %get-tuple-element.5.refs_1_), custom_call_target="tpu_custom_call" | custom-call | tf_op jit(solution)/shard_map/ortho/pallas_call | solution.py:552
Async XLA Ops:
  0.6 0.9 %copy-start = (s32[4,32,256]{2,1,0:T(8,128)S(1)}, s32[4,32,256]{2,1,0:T(8,128)}, u32[]{:S(2)}) copy-start(s32[4,32,256]{2,1,0:T(8,128)} %refs_1_.1) | copy-start | bytes 393220
  1.5 0.8 %copy-start.1 = (s32[32,256]{1,0:T(8,128)S(1)}, s32[32,256]{1,0:T(8,128)}, u32[]{:S(2)}) copy-start(s32[32,256]{1,0:T(8,128)} %refs_0_.1) | copy-start | bytes 98308

commit v2 on v1

--- a/solution.py
+++ b/solution.py
@@ -17,6 +17,7 @@
     (-1, 1, 3, 0, 1.0 / 18.0),
 )
 PANEL = 16
+VMEM_GRANT = 64 * 1024 * 1024
 
 
 DIRECTIONS = ((-1, 0), (1, 0), (0, -1), (0, 1), (-1, -1), (-1, 1), (1, -1), (1, 1))
@@ -84,16 +85,17 @@
     vectors, width = source.shape[1], source.shape[2]
     parts = [weights[n, pl.ds(weight_row, 1), :] for n in range(len(STEPS))]
     for base in range(0, vectors, CHUNK):
-        above = source[at - 1, base : base + CHUNK, :]
-        here = source[at, base : base + CHUNK, :]
-        below = source[at + 1, base : base + CHUNK, :]
-        from_left = parts[0] * above + parts[1] * here + parts[2] * below
-        from_right = parts[3] * above + parts[4] * here + parts[5] * below
-        upright = parts[6] * above + parts[7] * below
-        store(
-            base,
-            here - (upright + pltpu.roll(from_left, 1, 1) + pltpu.roll(from_right, width - 1, 1)),
-        )
+        done = []
+        for start in range(base, base + CHUNK, 8):
+            above = source[at - 1, start : start + 8, :]
+            here = source[at, start : start + 8, :]
+            below = source[at + 1, start : start + 8, :]
+            from_left = parts[0] * above + parts[1] * here + parts[2] * below
+            from_right = parts[3] * above + parts[4] * here + parts[5] * below
+            upright = parts[6] * above + parts[7] * below
+            sides = pltpu.roll(from_left, 1, 1) + pltpu.roll(from_right, width - 1, 1)
+            done.append(here - (upright + sides))
+        store(base, jnp.concatenate(done, axis=0))
 
 
 def filter_kernel(
@@ -289,13 +291,21 @@
         arrive(d, label_copies[d])
     stencil_weights(levels, counts, weights, row, col, row_count, col_count)
 
-    for d in range(2, 8):
+    def rims(start, stop, left, right):
+        for r in range(start, stop):
+            on_right = pltpu.roll(right, (-(EDGE + 2 * r)) % LANES, 1)
+            on_left = pltpu.roll(left, (LANES - 2 - EDGE - 2 * r) % LANES, 1)
+            wide[2 + r, :, cols:] = jnp.where(lane < LANES // 2, on_right, on_left)
+
+    for d in (2, 3):
         arrive(d, value_copies[d])
-    left, right = halo[0].T, halo[1].T
-    for r in range(-2, rows + 2):
-        on_right = pltpu.roll(right, (-(EDGE + 2 * r)) % LANES, 1)
-        on_left = pltpu.roll(left, (LANES - 2 - EDGE - 2 * r) % LANES, 1)
-        wide[2 + r, :, cols:] = jnp.where(lane < LANES // 2, on_right, on_left)
+    above_pad = jnp.zeros((EDGE, vectors), jnp.float32)
+    below_pad = jnp.zeros((LANES - EDGE - used, vectors), jnp.float32)
+    beside = [
+        jnp.concatenate([above_pad, halo[side, pl.ds(EDGE, used), :], below_pad], axis=0).T
+        for side in range(2)
+    ]
+    rims(0, rows, *beside)
 
     def first(m):
         def store(base, values):
@@ -320,21 +330,26 @@
     total[...] = jnp.zeros(total.shape, jnp.float32)
     first(2)
     first(3)
+    first(4)
+    second(2)
+
+    first(5)
 
     def inner(r, carry):
-        first(r + 2)
+        product(r - 1)
         second(r)
+        first(r + 3)
         return carry
 
-    lax.fori_loop(2, rows - 2, inner, 0)
-
-    def inner_product(r, carry):
-        product(r)
-        return carry
-
-    lax.fori_loop(2, rows - 2, inner_product, 0)
-    for d in range(2):
+    lax.fori_loop(3, rows - 3, inner, 0)
+    second(rows - 3)
+    product(rows - 4)
+    product(rows - 3)
+    for d in (0, 1, 4, 5, 6, 7):
         arrive(d, value_copies[d])
+    corner = [halo[0].T, halo[1].T]
+    rims(-2, 0, *corner)
+    rims(rows, rows + 2, *corner)
     for m in (0, 1, rows, rows + 1):
         first(m)
     for r in (0, 1, rows - 2, rows - 1):
@@ -457,7 +472,7 @@
             pltpu.SemaphoreType.DMA((swaps,)),
         ],
         compiler_params=pltpu.CompilerParams(
-            collective_id=0, has_side_effects=True, vmem_limit_bytes=48 * 1024 * 1024
+            collective_id=0, has_side_effects=True, vmem_limit_bytes=VMEM_GRANT
         ),
         name="filter",
     )(intensity, agreement, basis_block)
@@ -570,7 +585,7 @@
             pltpu.SemaphoreType.DMA,
             pltpu.SemaphoreType.DMA((rows // 8,)),
         ],
-        compiler_params=pltpu.CompilerParams(vmem_limit_bytes=40 * 1024 * 1024),
+        compiler_params=pltpu.CompilerParams(vmem_limit_bytes=VMEM_GRANT),
         name="ortho",
     )(gram, filt)
 

time: 64.5 us -> 47.7 us (0.74)
  Pallas kernels: 61.9 us -> 46.8 us
  local copies, waits for them, and re-layouts: 1.65 us -> 0 us
    pallas_call x1, Pallas kernels: 52.1 us -> 36.4 us  [filter_call(): pl.pallas_call(body, out_shape=(jax.ShapeDtypeStruct((rows, 2 * vectors,...]
    unnamed x4 -> x0, local copies, waits for them, and re-layouts: 1.65 us -> none
where the time goes in v2:
time: 47.7 us; the launch traced here: 47.6 us
  Pallas kernels  46.8 us (98%)
  between operations  0.8 us (2%)
    pallas_call x1, Pallas kernels, filter_call(): pl.pallas_call(body, out_shape=(jax.ShapeDtypeStruct((rows, 2 * vectors,...  36.4 us
    pallas_call x1, Pallas kernels, ortho_call(): pl.pallas_call(body, out_shape=(jax.ShapeDtypeStruct((vectors, rows, cols...  10.4 us

profile of v2, /device:TPU:0, one launch (start us, length us, event | category | flops | bytes accessed | tf_op | source)
XLA Modules:
  0.0 47.6 jit_solution(16607197575580299848)
XLA Ops:
  0.6 36.4 %filter.1 = (bf16[32,256,256]{2,1,0:T(8,128)(2,1)}, f32[128,128]{1,0:T(8,128)}) custom-call(s32[32,256]{1,0:T(8,128)} %refs_0_.1, s32[4,32,256]{2,1,0:T(8,128)} %refs_1_.1, f32[128,32,256]{2,1,0:T(8,128)} %refs_2_.1), custom_call_target="tpu_custom_call" | custom-call | tf_op jit(solution)/shard_map/filter/pallas_call | solution.py:445
  37.0 10.4 %ortho.1 = (f32[128,32,256]{2,1,0:T(8,128)}, f32[128,128]{1,0:T(8,128)}) custom-call(f32[128,128]{1,0:T(8,128)} %get-tuple-element.4.refs_0_, bf16[32,256,256]{2,1,0:T(8,128)(2,1)} %get-tuple-element.5.refs_1_), custom_call_target="tpu_custom_call" | custom-call | tf_op jit(solution)/shard_map/ortho/pallas_call | solution.py:567

commit v3 on v2

--- a/solution.py
+++ b/solution.py
@@ -321,30 +321,34 @@
 
         apply_row(middle, r + 1, weights, r + EDGE, store)
 
-    def product(r):
-        pair = pairs[r]
+    def product(r, s):
+        pair = jnp.concatenate([pairs[r], pairs[s]], axis=1)
         total[...] += lax.dot_general(
             pair, pair, (((1,), (1,)), ((), ())), preferred_element_type=jnp.float32
         )
 
     total[...] = jnp.zeros(total.shape, jnp.float32)
-    first(2)
-    first(3)
-    first(4)
+    for m in range(2, 6):
+        first(m)
     second(2)
-
-    first(5)
-
-    def inner(r, carry):
-        product(r - 1)
+    second(3)
+    first(6)
+    first(7)
+
+    def inner(i, carry):
+        r = 4 + 2 * i
+        product(r - 2, r - 1)
         second(r)
-        first(r + 3)
+        second(r + 1)
+        first(r + 4)
+        first(r + 5)
         return carry
 
-    lax.fori_loop(3, rows - 3, inner, 0)
+    lax.fori_loop(0, (rows - 8) // 2, inner, 0)
+    product(rows - 6, rows - 5)
+    second(rows - 4)
     second(rows - 3)
-    product(rows - 4)
-    product(rows - 3)
+    product(rows - 4, rows - 3)
     for d in (0, 1, 4, 5, 6, 7):
         arrive(d, value_copies[d])
     corner = [halo[0].T, halo[1].T]
@@ -356,8 +360,8 @@
         second(r)
     keep = pltpu.make_async_copy(pairs, pair_out, local_sem.at[groups + 2])
     keep.start()
-    for r in (0, 1, rows - 2, rows - 1):
-        product(r)
+    product(0, 1)
+    product(rows - 2, rows - 1)
 
     block = vectors // col_count
     share[...] = (total[:vectors, :vectors] + total[vectors:, vectors:]) + (
@@ -482,39 +486,39 @@
     size, width = work.shape
     for base in range(0, size, PANEL):
         block = work[pl.ds(base, PANEL), :]
-        rows = [block[i : i + 1, :] for i in range(PANEL)]
+        rows = [
+            [block[i : i + 1, side : side + LANES] for side in range(0, width, LANES)]
+            for i in range(PANEL)
+        ]
         pivots = [
             [
                 None
                 if k < i
-                else jnp.broadcast_to(rows[i][:, base + k : base + k + 1], (1, width))
+                else jnp.broadcast_to(block[i : i + 1, base + k : base + k + 1], (1, LANES))
                 for k in range(PANEL)
             ]
             for i in range(PANEL)
         ]
         for i in range(PANEL):
             inverse = lax.rsqrt(pivots[i][i])
-            rows[i] = rows[i] * inverse
+            rows[i] = [half * inverse for half in rows[i]]
             lead = [None if k <= i else pivots[i][k] * inverse for k in range(PANEL)]
             for k in range(i + 1, PANEL):
                 for m in range(k, PANEL):
                     pivots[k][m] = pivots[k][m] - lead[k] * lead[m]
             for k in range(i + 1, PANEL):
-                rows[k] = rows[k] - lead[k] * rows[i]
-        done = jnp.concatenate(rows, axis=0)
+                rows[k] = [half - lead[k] * done for half, done in zip(rows[k], rows[i])]
+        done = jnp.concatenate([jnp.concatenate(halves, axis=1) for halves in rows], axis=0)
         work[pl.ds(base, PANEL), :] = done
         rest = size - base - PANEL
         if rest > 0:
-            change = lax.dot_general(
-                done[:, :size].T,
+            change = jnp.dot(
+                done[:, :size].T[base + PANEL :],
                 done,
-                (((1,), (0,)), ((), ())),
                 precision=lax.Precision.HIGHEST,
                 preferred_element_type=jnp.float32,
             )
-            work[pl.ds(base + PANEL, rest), :] = (
-                work[pl.ds(base + PANEL, rest), :] - change[base + PANEL :, :]
-            )
+            work[pl.ds(base + PANEL, rest), :] = work[pl.ds(base + PANEL, rest), :] - change
 
 
 def split_two(values):

time: 47.7 us -> 46.9 us (0.983)
  Pallas kernels: 46.8 us -> 45.9 us
    pallas_call x1, Pallas kernels: 10.4 us -> 9.77 us  [ortho_call(): pl.pallas_call(body, out_shape=(jax.ShapeDtypeStruct((vectors, rows, cols...]
where the time goes in v3:
time: 46.9 us; the launch traced here: 46.7 us
  Pallas kernels  45.9 us (98%)
  between operations  0.8 us (2%)
    pallas_call x1, Pallas kernels, filter_call(): pl.pallas_call(body, out_shape=(jax.ShapeDtypeStruct((rows, 2 * vectors,...  36.1 us
    pallas_call x1, Pallas kernels, ortho_call(): pl.pallas_call(body, out_shape=(jax.ShapeDtypeStruct((vectors, rows, cols...  9.77 us

profile of v3, /device:TPU:0, one launch (start us, length us, event | category | flops | bytes accessed | tf_op | source)
XLA Modules:
  0.0 46.7 jit_solution(9614498695829441417)
XLA Ops:
  0.6 36.1 %filter.1 = (bf16[32,256,256]{2,1,0:T(8,128)(2,1)}, f32[128,128]{1,0:T(8,128)}) custom-call(s32[32,256]{1,0:T(8,128)} %refs_0_.1, s32[4,32,256]{2,1,0:T(8,128)} %refs_1_.1, f32[128,32,256]{2,1,0:T(8,128)} %refs_2_.1), custom_call_target="tpu_custom_call" | custom-call | tf_op jit(solution)/shard_map/filter/pallas_call | solution.py:449
  36.8 9.8 %ortho.1 = (f32[128,32,256]{2,1,0:T(8,128)}, f32[128,128]{1,0:T(8,128)}) custom-call(f32[128,128]{1,0:T(8,128)} %get-tuple-element.4.refs_0_, bf16[32,256,256]{2,1,0:T(8,128)(2,1)} %get-tuple-element.5.refs_1_), custom_call_target="tpu_custom_call" | custom-call | tf_op jit(solution)/shard_map/ortho/pallas_call | solution.py:571

commit v4 on v3

--- a/solution.py
+++ b/solution.py
@@ -184,6 +184,14 @@
         def _(step=step):
             greet(device(*step))
 
+    def turn(g):
+        fetches[g].wait()
+        wide[pl.ds(2 + 8 * g, 8), :, pl.ds(0, cols)] = jnp.swapaxes(
+            natural[:, pl.ds(8 * g, 8), :], 0, 1
+        )
+
+    turn(0)
+    turn(groups - 1)
     pl.semaphore_wait(barrier, col_count + row_count - 2 + corners)
 
     def span(step, size, edge):
@@ -237,20 +245,12 @@
         )
         launch(d, label_copies[d])
 
-    def turn(g):
-        fetches[g].wait()
-        wide[pl.ds(2 + 8 * g, 8), :, pl.ds(0, cols)] = jnp.swapaxes(
-            natural[:, pl.ds(8 * g, 8), :], 0, 1
-        )
-
-    turn(0)
     value_copies = [None] * 8
     value_copies[0] = [
         remote(wide.at[pl.ds(2, 2), :, pl.ds(0, cols)],
                wide.at[pl.ds(rows + 2, 2), :, pl.ds(0, cols)], 2, 0)
     ]
     launch(0, value_copies[0])
-    turn(groups - 1)
     value_copies[1] = [
         remote(wide.at[pl.ds(rows, 2), :, pl.ds(0, cols)],
                wide.at[pl.ds(0, 2), :, pl.ds(0, cols)], 2, 1)

time: 46.9 us -> 46.9 us (level)
  no operation moved by 1% of the time
where the time goes in v4:
time: 46.9 us; the launch traced here: 46.7 us
  Pallas kernels  45.9 us (98%)
  between operations  0.8 us (2%)
    pallas_call x1, Pallas kernels, filter_call(): pl.pallas_call(body, out_shape=(jax.ShapeDtypeStruct((rows, 2 * vectors,...  36.1 us
    pallas_call x1, Pallas kernels, ortho_call(): pl.pallas_call(body, out_shape=(jax.ShapeDtypeStruct((vectors, rows, cols...  9.77 us

profile of v4, /device:TPU:0, one launch (start us, length us, event | category | flops | bytes accessed | tf_op | source)
XLA Modules:
  0.0 46.7 jit_solution(16810473238629518478)
XLA Ops:
  0.6 36.1 %filter.1 = (bf16[32,256,256]{2,1,0:T(8,128)(2,1)}, f32[128,128]{1,0:T(8,128)}) custom-call(s32[32,256]{1,0:T(8,128)} %refs_0_.1, s32[4,32,256]{2,1,0:T(8,128)} %refs_1_.1, f32[128,32,256]{2,1,0:T(8,128)} %refs_2_.1), custom_call_target="tpu_custom_call" | custom-call | tf_op jit(solution)/shard_map/filter/pallas_call | solution.py:449
  36.8 9.8 %ortho.1 = (f32[128,32,256]{2,1,0:T(8,128)}, f32[128,128]{1,0:T(8,128)}) custom-call(f32[128,128]{1,0:T(8,128)} %get-tuple-element.4.refs_0_, bf16[32,256,256]{2,1,0:T(8,128)(2,1)} %get-tuple-element.5.refs_1_), custom_call_target="tpu_custom_call" | custom-call | tf_op jit(solution)/shard_map/ortho/pallas_call | solution.py:571
